TPU v7x, 32 devices: a whole 2x2x4 slice. The times are simulated.
32 devices in a mesh: section: 8 (over z, core), req: 4 (over y, x).
Axes of the slice: x: 2, y: 2, z: 4, core: 2. Of those that a mesh axis runs over, the one named last changes fastest.
Arguments:
- latents: bfloat16 [128, 3072], P('req'), may hold values from -6 to 6
- patch_route: int32 [128], replicated, may hold values from 0 to 127, each once
- request_len: int32 [16], replicated, may hold values from 1 to 32, 128 in all
- span_order: int32 [2], replicated, may hold values from 0 to 1, each once
- modulation: float32 [8, 16, 3, 3072], P('section'), may hold values from -4 to 4
- w_qkv: bfloat16 [8, 3072, 16, 384], P('section', None, 'req'), may hold values from -0.109375 to 0.109375
- w_mlp_in: bfloat16 [8, 3072, 6144], P('section', None, 'req'), may hold values from -0.109375 to 0.109375
- w_out_attn: bfloat16 [8, 16, 128, 3072], P('section', 'req'), may hold values from -0.0625 to 0.0625
- w_out_mlp: bfloat16 [8, 6144, 3072], P('section', 'req'), may hold values from -0.0625 to 0.0625
- stale_kv: bfloat16 [8, 128, 16, 256], P('section', None, 'req'), may hold values from -160 to 160
Outputs:
- denoised: bfloat16 [128, 3072], P('req', 'section')
All inputs are finite; a program needn't handle non-finite values.
Results may differ from a plain program's by a relative error of at most 0.04.
Values may be sent and summed in bfloat16 or wider, within the bound.
A program may use at most 128 MiB of HBM per device.

v0:
```python
import jax
import jax.numpy as jnp
from jax import lax
from jax.sharding import PartitionSpec as P


def from_behind(block, axis, distance):
    devices = range(lax.axis_size(axis))
    route = [(i - distance, i) for i in devices if i - distance in devices]
    return lax.ppermute(block, axis, route)


def spread_2(value, axis, source):
    kept = jnp.where(lax.axis_index(axis) == source, value, 0).astype(value.dtype)
    return lax.psum(kept, axis)


def layer_norm(values):
    row_mean = jnp.mean(values, axis=-1, keepdims=True)
    centered = values - row_mean
    row_var = jnp.mean(centered * centered, axis=-1, keepdims=True)
    return centered * lax.rsqrt(row_var + 1e-06)


def gelu_tanh(values):
    return (
        0.5
        * values
        * (1.0 + jnp.tanh(0.7978845608028654 * (values + 0.044715 * values * values * values)))
    )


def shards(
    latents,
    patch_route,
    request_len,
    span_order,
    modulation,
    w_qkv,
    w_mlp_in,
    w_out_attn,
    w_out_mlp,
    stale_kv,
):
    section_count = lax.axis_size("section")
    req_count = lax.axis_size("req")
    section_index = lax.axis_index("section")
    req_index = lax.axis_index("req")
    patches = patch_route.shape[0]
    span_count = span_order.shape[0]
    span_rows = patches // span_count
    model_width = latents.shape[1]
    col_width = model_width // req_count
    section_cols = model_width // section_count
    req_total = request_len.shape[0]
    heads_dev = w_qkv.shape[2]
    head_dim = w_qkv.shape[3] // 3
    starts = jnp.cumsum(request_len) - request_len
    patch_ids = jnp.arange(patches, dtype=jnp.int32)
    owner_req = jnp.sum((patch_ids[:, None] >= starts[None, :]).astype(jnp.int32), axis=1) - 1
    seq_req = owner_req[patch_route]
    req_ids = jnp.arange(req_total, dtype=jnp.int32)
    mod_table = modulation[0].reshape(req_total, 3 * model_width)
    qkv_weight = w_qkv[0].reshape(model_width, heads_dev * 3 * head_dim)
    mlp_weight = w_mlp_in[0]
    attn_out_weight = w_out_attn[0].reshape(heads_dev * head_dim, model_width)
    mlp_out_weight = w_out_mlp[0]
    spread = lax.all_to_all(latents, "req", split_axis=1, concat_axis=0, tiled=True)
    sequence = spread[patch_route]
    in_width = sequence.shape[1]

    def work(incoming, kv_cache, span_id):
        first_row = span_id * span_rows
        row_req = lax.dynamic_slice_in_dim(seq_req, first_row, span_rows, 0)
        onehot = (row_req[:, None] == req_ids[None, :]).astype(jnp.float32)
        mod_rows = jnp.dot(onehot, mod_table, precision=lax.Precision.HIGHEST).reshape(
            span_rows, 3, model_width
        )
        current = lax.all_gather(incoming, "req", axis=1, tiled=True)
        normed = (
            layer_norm(current.astype(jnp.float32)) * (1.0 + mod_rows[:, 1]) + mod_rows[:, 0]
        ).astype(jnp.bfloat16)
        qkv_rows = jnp.dot(normed, qkv_weight, preferred_element_type=jnp.float32).reshape(
            span_rows, heads_dev, 3 * head_dim
        )
        query_rows = qkv_rows[:, :, :head_dim].astype(jnp.bfloat16)
        fresh_kv = qkv_rows[:, :, head_dim:].astype(jnp.bfloat16)
        kv_cache = lax.dynamic_update_slice_in_dim(kv_cache, fresh_kv, first_row, 0)
        key_rows = kv_cache[:, :, :head_dim]
        value_rows = kv_cache[:, :, head_dim:]
        scores = jnp.einsum(
            "chd,phd->hcp", query_rows, key_rows, preferred_element_type=jnp.float32
        ) / jnp.sqrt(jnp.float32(head_dim))
        same_req = row_req[:, None] == seq_req[None, :]
        scores = jnp.where(same_req[None], scores, -jnp.inf)
        row_top = jnp.max(scores, axis=-1, keepdims=True)
        weights = jnp.exp(scores - row_top)
        weight_sum = jnp.sum(weights, axis=-1, keepdims=True)
        attention = (weights / weight_sum).astype(jnp.bfloat16)
        attended = jnp.einsum(
            "hcp,phd->chd", attention, value_rows, preferred_element_type=jnp.float32
        ).astype(jnp.bfloat16)
        attended = attended.reshape(span_rows, heads_dev * head_dim)
        mlp_act = gelu_tanh(jnp.dot(normed, mlp_weight, preferred_element_type=jnp.float32)).astype(
            jnp.bfloat16
        )
        partial_value = jnp.dot(attended, attn_out_weight, preferred_element_type=jnp.float32)
        partial_value = partial_value + jnp.dot(
            mlp_act, mlp_out_weight, preferred_element_type=jnp.float32
        )
        branch = lax.psum_scatter(
            partial_value.astype(jnp.bfloat16), "req", scatter_dimension=1, tiled=True
        ).astype(jnp.float32)
        gate_cols = lax.dynamic_slice_in_dim(mod_rows[:, 2], req_index * col_width, col_width, 1)
        updated = (incoming.astype(jnp.float32) + gate_cols * branch).astype(jnp.bfloat16)
        return (updated, kv_cache)

    def advance(moment, carry):
        incoming, kv_cache, results = carry
        span_slot = moment - section_index
        active = (span_slot >= 0) & (span_slot < span_count)
        span_id = span_order[jnp.clip(span_slot, 0, span_count - 1)]
        first_row = span_id * span_rows
        entering = lax.dynamic_slice_in_dim(sequence, first_row, span_rows, 0)
        source = jnp.where(section_index == 0, entering, incoming)
        computed, new_cache = work(source, kv_cache, span_id)
        updated = jnp.where(active, computed, jnp.zeros_like(computed))
        kv_cache = jnp.where(active, new_cache, kv_cache)
        store_here = active & (section_index == section_count - 1)
        current = lax.dynamic_slice_in_dim(results, first_row, span_rows, 0)
        results = lax.dynamic_update_slice_in_dim(
            results, jnp.where(store_here, updated, current), first_row, 0
        )
        incoming = from_behind(updated, "section", 1)
        return (incoming, kv_cache, results)

    start_state = (
        jnp.zeros((span_rows, in_width), jnp.bfloat16),
        stale_kv[0],
        jnp.zeros((patches, in_width), jnp.bfloat16),
    )
    last_in, last_cache, results = lax.fori_loop(
        0, span_count + section_count - 1, advance, start_state
    )
    finished = spread_2(results, "section", section_count - 1)
    inverse = jnp.zeros((patches,), jnp.int32).at[patch_route].set(patch_ids)
    unrouted = finished[inverse]
    owned = lax.all_to_all(unrouted, "req", split_axis=0, concat_axis=1, tiled=True)
    return lax.dynamic_slice_in_dim(owned, section_index * section_cols, section_cols, 1)


def solution(mesh):
    in_specs = (
        P("req", None),
        P(),
        P(),
        P(),
        P("section", None, None, None),
        P("section", None, "req", None),
        P("section", None, "req"),
        P("section", "req", None, None),
        P("section", "req", None),
        P("section", None, "req", None),
    )
    out_specs = P("req", "section")
    return jax.shard_map(shards, mesh=mesh, in_specs=in_specs, out_specs=out_specs, check_vma=False)
```

profile of v0, /device:TPU:1, one launch (start us, length us, event | category | flops | bytes accessed | tf_op | source)
XLA Modules:
  0.0 801.5 jit_solution(6985805251683365156)
XLA Ops:
  9.0 4.3 all-to-all-start
  15.6 9.0 %copy.49 = bf16[384,8,4,384]{3,1,2,0:T(8,128)(2,1)} copy(bf16[384,8,4,384]{3,2,1,0:T(4,128)(2,1)} %bitcast.96) | data formatting | bytes 18874368
  30.9 696.5 %while.20 = (s32[]{:T(128)}, bf16[64,768]{1,0:T(8,128)(2,1)S(1)}, bf16[128,4,256]{2,0,1:T(8,128)(2,1)S(1)}, bf16[128,768]{1,0:T(8,128)(2,1)}, s32[]{:T(128)}, /*...) while((s32[]{:T(128)}, bf16[64,768]{1,0:T(8,128)(2,1)S(1)}, ...), condition=%wide.region_8.9_spmd.clone, body=%wide.region_2.8_spmd.clone.sunk | while | flops 2149393920 | bytes 57825944 | solution.py:142
  33.2 8.4 %all_gather.11 = bf16[64,3072]{1,0:T(8,128)(2,1)S(1)} all-gather(bf16[64,768]{1,0:T(8,128)(2,1)S(1)} %dynamic-slice_select_fusion.2), channel_id=1, replica_groups=mesh['section'=8,'req'=4] {'req'}, dimensions={1}, use_global_device_ids=true | all-gather | bytes 491520 | tf_op jit(solution)/shard_map/while/body/eval_jaxpr/all_gather | solution.py:79
  44.3 3.1 reshape.163
  47.4 7.2 fusion.96
  54.7 5.5 convolution_convert_fusion.3
  63.9 10.6 %fusion.102 = bf16[64,3072]{1,0:T(8,128)(2,1)} fusion(f32[64,3072]{1,0:T(8,128)S(1)} %fusion.101, bf16[1536,3072]{1,0:T(8,128)(2,1)} %get-tuple-element.592, bf16[3072,1536]{1,0:T(8,128)(2,1)} %get-tuple-element.591, bf16[64,3072]{1,0:T(8,128)(2,1)S(1)} %all_gather.11, f32[64,1,3072]{2,1,0:T(1,128)S(1)} %get-tuple-element.531, ...), kind=kOutput, calls=%fused_computation.7.clone.1 | convolution fusion | flops 1210613760 | bytes 22020608 | tf_op jit(solution)/shard_map/while/body/eval_jaxpr/dot_general | solution.py:108
  75.5 26.5 %reduce-scatter.2.cloned.1.call-done = bf16[64,768]{1,0:T(8,128)(2,1)} async-done(((bf16[64,3072]{1,0:T(8,128)(2,1)}), bf16[64,768]{1,0:T(8,128)(2,1)}) %reduce-scatter.2.cloned.1.call-update) | async-done | bytes 98320 | tf_op jit(solution)/shard_map/while/body/eval_jaxpr/reduce_scatter | solution.py:111
  103.6 4.0 collective-permute-start
  111.4 8.5 %all_gather.11 = bf16[64,3072]{1,0:T(8,128)(2,1)S(1)} all-gather(bf16[64,768]{1,0:T(8,128)(2,1)S(1)} %dynamic-slice_select_fusion.2), channel_id=1, replica_groups=mesh['section'=8,'req'=4] {'req'}, dimensions={1}, use_global_device_ids=true | all-gather | bytes 491520 | tf_op jit(solution)/shard_map/while/body/eval_jaxpr/all_gather | solution.py:79
  122.6 3.1 reshape.163
  125.7 7.2 fusion.96
  133.0 5.5 convolution_convert_fusion.3
  142.2 10.6 %fusion.102 = bf16[64,3072]{1,0:T(8,128)(2,1)} fusion(f32[64,3072]{1,0:T(8,128)S(1)} %fusion.101, bf16[1536,3072]{1,0:T(8,128)(2,1)} %get-tuple-element.592, bf16[3072,1536]{1,0:T(8,128)(2,1)} %get-tuple-element.591, bf16[64,3072]{1,0:T(8,128)(2,1)S(1)} %all_gather.11, f32[64,1,3072]{2,1,0:T(1,128)S(1)} %get-tuple-element.531, ...), kind=kOutput, calls=%fused_computation.7.clone.1 | convolution fusion | flops 1210613760 | bytes 22020608 | tf_op jit(solution)/shard_map/while/body/eval_jaxpr/dot_general | solution.py:108
  153.9 25.4 %reduce-scatter.2.cloned.1.call-done = bf16[64,768]{1,0:T(8,128)(2,1)} async-done(((bf16[64,3072]{1,0:T(8,128)(2,1)}), bf16[64,768]{1,0:T(8,128)(2,1)}) %reduce-scatter.2.cloned.1.call-update) | async-done | bytes 98320 | tf_op jit(solution)/shard_map/while/body/eval_jaxpr/reduce_scatter | solution.py:111
  180.9 4.0 collective-permute-start
  188.7 8.5 %all_gather.11 = bf16[64,3072]{1,0:T(8,128)(2,1)S(1)} all-gather(bf16[64,768]{1,0:T(8,128)(2,1)S(1)} %dynamic-slice_select_fusion.2), channel_id=1, replica_groups=mesh['section'=8,'req'=4] {'req'}, dimensions={1}, use_global_device_ids=true | all-gather | bytes 491520 | tf_op jit(solution)/shard_map/while/body/eval_jaxpr/all_gather | solution.py:79
  199.9 3.1 reshape.163
  203.0 7.2 fusion.96
  210.3 5.5 convolution_convert_fusion.3
  219.5 10.6 %fusion.102 = bf16[64,3072]{1,0:T(8,128)(2,1)} fusion(f32[64,3072]{1,0:T(8,128)S(1)} %fusion.101, bf16[1536,3072]{1,0:T(8,128)(2,1)} %get-tuple-element.592, bf16[3072,1536]{1,0:T(8,128)(2,1)} %get-tuple-element.591, bf16[64,3072]{1,0:T(8,128)(2,1)S(1)} %all_gather.11, f32[64,1,3072]{2,1,0:T(1,128)S(1)} %get-tuple-element.531, ...), kind=kOutput, calls=%fused_computation.7.clone.1 | convolution fusion | flops 1210613760 | bytes 22020608 | tf_op jit(solution)/shard_map/while/body/eval_jaxpr/dot_general | solution.py:108
  231.1 25.4 %reduce-scatter.2.cloned.1.call-done = bf16[64,768]{1,0:T(8,128)(2,1)} async-done(((bf16[64,3072]{1,0:T(8,128)(2,1)}), bf16[64,768]{1,0:T(8,128)(2,1)}) %reduce-scatter.2.cloned.1.call-update) | async-done | bytes 98320 | tf_op jit(solution)/shard_map/while/body/eval_jaxpr/reduce_scatter | solution.py:111
  258.2 4.0 collective-permute-start
  266.0 8.5 %all_gather.11 = bf16[64,3072]{1,0:T(8,128)(2,1)S(1)} all-gather(bf16[64,768]{1,0:T(8,128)(2,1)S(1)} %dynamic-slice_select_fusion.2), channel_id=1, replica_groups=mesh['section'=8,'req'=4] {'req'}, dimensions={1}, use_global_device_ids=true | all-gather | bytes 491520 | tf_op jit(solution)/shard_map/while/body/eval_jaxpr/all_gather | solution.py:79
  280.3 7.2 fusion.96
  287.5 5.5 convolution_convert_fusion.3
  296.8 10.6 %fusion.102 = bf16[64,3072]{1,0:T(8,128)(2,1)} fusion(f32[64,3072]{1,0:T(8,128)S(1)} %fusion.101, bf16[1536,3072]{1,0:T(8,128)(2,1)} %get-tuple-element.592, bf16[3072,1536]{1,0:T(8,128)(2,1)} %get-tuple-element.591, bf16[64,3072]{1,0:T(8,128)(2,1)S(1)} %all_gather.11, f32[64,1,3072]{2,1,0:T(1,128)S(1)} %get-tuple-element.531, ...), kind=kOutput, calls=%fused_computation.7.clone.1 | convolution fusion | flops 1210613760 | bytes 22020608 | tf_op jit(solution)/shard_map/while/body/eval_jaxpr/dot_general | solution.py:108
  308.4 25.4 %reduce-scatter.2.cloned.1.call-done = bf16[64,768]{1,0:T(8,128)(2,1)} async-done(((bf16[64,3072]{1,0:T(8,128)(2,1)}), bf16[64,768]{1,0:T(8,128)(2,1)}) %reduce-scatter.2.cloned.1.call-update) | async-done | bytes 98320 | tf_op jit(solution)/shard_map/while/body/eval_jaxpr/reduce_scatter | solution.py:111
  335.5 4.0 collective-permute-start
  343.3 8.5 %all_gather.11 = bf16[64,3072]{1,0:T(8,128)(2,1)S(1)} all-gather(bf16[64,768]{1,0:T(8,128)(2,1)S(1)} %dynamic-slice_select_fusion.2), channel_id=1, replica_groups=mesh['section'=8,'req'=4] {'req'}, dimensions={1}, use_global_device_ids=true | all-gather | bytes 491520 | tf_op jit(solution)/shard_map/while/body/eval_jaxpr/all_gather | solution.py:79
  357.6 7.2 fusion.96
  364.8 5.5 convolution_convert_fusion.3
  374.0 10.6 %fusion.102 = bf16[64,3072]{1,0:T(8,128)(2,1)} fusion(f32[64,3072]{1,0:T(8,128)S(1)} %fusion.101, bf16[1536,3072]{1,0:T(8,128)(2,1)} %get-tuple-element.592, bf16[3072,1536]{1,0:T(8,128)(2,1)} %get-tuple-element.591, bf16[64,3072]{1,0:T(8,128)(2,1)S(1)} %all_gather.11, f32[64,1,3072]{2,1,0:T(1,128)S(1)} %get-tuple-element.531, ...), kind=kOutput, calls=%fused_computation.7.clone.1 | convolution fusion | flops 1210613760 | bytes 22020608 | tf_op jit(solution)/shard_map/while/body/eval_jaxpr/dot_general | solution.py:108
  385.7 25.4 %reduce-scatter.2.cloned.1.call-done = bf16[64,768]{1,0:T(8,128)(2,1)} async-done(((bf16[64,3072]{1,0:T(8,128)(2,1)}), bf16[64,768]{1,0:T(8,128)(2,1)}) %reduce-scatter.2.cloned.1.call-update) | async-done | bytes 98320 | tf_op jit(solution)/shard_map/while/body/eval_jaxpr/reduce_scatter | solution.py:111
  412.8 4.0 collective-permute-start
  420.6 8.5 %all_gather.11 = bf16[64,3072]{1,0:T(8,128)(2,1)S(1)} all-gather(bf16[64,768]{1,0:T(8,128)(2,1)S(1)} %dynamic-slice_select_fusion.2), channel_id=1, replica_groups=mesh['section'=8,'req'=4] {'req'}, dimensions={1}, use_global_device_ids=true | all-gather | bytes 491520 | tf_op jit(solution)/shard_map/while/body/eval_jaxpr/all_gather | solution.py:79
  431.8 3.1 reshape.163
  434.9 7.2 fusion.96
  442.1 5.5 convolution_convert_fusion.3
  451.4 10.6 %fusion.102 = bf16[64,3072]{1,0:T(8,128)(2,1)} fusion(f32[64,3072]{1,0:T(8,128)S(1)} %fusion.101, bf16[1536,3072]{1,0:T(8,128)(2,1)} %get-tuple-element.592, bf16[3072,1536]{1,0:T(8,128)(2,1)} %get-tuple-element.591, bf16[64,3072]{1,0:T(8,128)(2,1)S(1)} %all_gather.11, f32[64,1,3072]{2,1,0:T(1,128)S(1)} %get-tuple-element.531, ...), kind=kOutput, calls=%fused_computation.7.clone.1 | convolution fusion | flops 1210613760 | bytes 22020608 | tf_op jit(solution)/shard_map/while/body/eval_jaxpr/dot_general | solution.py:108
  463.0 25.4 %reduce-scatter.2.cloned.1.call-done = bf16[64,768]{1,0:T(8,128)(2,1)} async-done(((bf16[64,3072]{1,0:T(8,128)(2,1)}), bf16[64,768]{1,0:T(8,128)(2,1)}) %reduce-scatter.2.cloned.1.call-update) | async-done | bytes 98320 | tf_op jit(solution)/shard_map/while/body/eval_jaxpr/reduce_scatter | solution.py:111
  490.1 4.0 collective-permute-start
  497.8 8.5 %all_gather.11 = bf16[64,3072]{1,0:T(8,128)(2,1)S(1)} all-gather(bf16[64,768]{1,0:T(8,128)(2,1)S(1)} %dynamic-slice_select_fusion.2), channel_id=1, replica_groups=mesh['section'=8,'req'=4] {'req'}, dimensions={1}, use_global_device_ids=true | all-gather | bytes 491520 | tf_op jit(solution)/shard_map/while/body/eval_jaxpr/all_gather | solution.py:79
  512.1 7.2 fusion.96
  519.4 5.5 convolution_convert_fusion.3
  528.6 10.6 %fusion.102 = bf16[64,3072]{1,0:T(8,128)(2,1)} fusion(f32[64,3072]{1,0:T(8,128)S(1)} %fusion.101, bf16[1536,3072]{1,0:T(8,128)(2,1)} %get-tuple-element.592, bf16[3072,1536]{1,0:T(8,128)(2,1)} %get-tuple-element.591, bf16[64,3072]{1,0:T(8,128)(2,1)S(1)} %all_gather.11, f32[64,1,3072]{2,1,0:T(1,128)S(1)} %get-tuple-element.531, ...), kind=kOutput, calls=%fused_computation.7.clone.1 | convolution fusion | flops 1210613760 | bytes 22020608 | tf_op jit(solution)/shard_map/while/body/eval_jaxpr/dot_general | solution.py:108
  540.3 25.4 %reduce-scatter.2.cloned.1.call-done = bf16[64,768]{1,0:T(8,128)(2,1)} async-done(((bf16[64,3072]{1,0:T(8,128)(2,1)}), bf16[64,768]{1,0:T(8,128)(2,1)}) %reduce-scatter.2.cloned.1.call-update) | async-done | bytes 98320 | tf_op jit(solution)/shard_map/while/body/eval_jaxpr/reduce_scatter | solution.py:111
  567.3 4.0 collective-permute-start
  575.2 8.4 %all_gather.11 = bf16[64,3072]{1,0:T(8,128)(2,1)S(1)} all-gather(bf16[64,768]{1,0:T(8,128)(2,1)S(1)} %dynamic-slice_select_fusion.2), channel_id=1, replica_groups=mesh['section'=8,'req'=4] {'req'}, dimensions={1}, use_global_device_ids=true | all-gather | bytes 491520 | tf_op jit(solution)/shard_map/while/body/eval_jaxpr/all_gather | solution.py:79
  589.4 7.2 fusion.96
  596.7 5.5 convolution_convert_fusion.3
  605.9 10.6 %fusion.102 = bf16[64,3072]{1,0:T(8,128)(2,1)} fusion(f32[64,3072]{1,0:T(8,128)S(1)} %fusion.101, bf16[1536,3072]{1,0:T(8,128)(2,1)} %get-tuple-element.592, bf16[3072,1536]{1,0:T(8,128)(2,1)} %get-tuple-element.591, bf16[64,3072]{1,0:T(8,128)(2,1)S(1)} %all_gather.11, f32[64,1,3072]{2,1,0:T(1,128)S(1)} %get-tuple-element.531, ...), kind=kOutput, calls=%fused_computation.7.clone.1 | convolution fusion | flops 1210613760 | bytes 22020608 | tf_op jit(solution)/shard_map/while/body/eval_jaxpr/dot_general | solution.py:108
  617.6 25.4 %reduce-scatter.2.cloned.1.call-done = bf16[64,768]{1,0:T(8,128)(2,1)} async-done(((bf16[64,3072]{1,0:T(8,128)(2,1)}), bf16[64,768]{1,0:T(8,128)(2,1)}) %reduce-scatter.2.cloned.1.call-update) | async-done | bytes 98320 | tf_op jit(solution)/shard_map/while/body/eval_jaxpr/reduce_scatter | solution.py:111
  644.6 4.0 collective-permute-start
  652.4 8.5 %all_gather.11 = bf16[64,3072]{1,0:T(8,128)(2,1)S(1)} all-gather(bf16[64,768]{1,0:T(8,128)(2,1)S(1)} %dynamic-slice_select_fusion.2), channel_id=1, replica_groups=mesh['section'=8,'req'=4] {'req'}, dimensions={1}, use_global_device_ids=true | all-gather | bytes 491520 | tf_op jit(solution)/shard_map/while/body/eval_jaxpr/all_gather | solution.py:79
  666.7 7.2 fusion.96
  674.0 5.5 convolution_convert_fusion.3
  683.2 10.6 %fusion.102 = bf16[64,3072]{1,0:T(8,128)(2,1)} fusion(f32[64,3072]{1,0:T(8,128)S(1)} %fusion.101, bf16[1536,3072]{1,0:T(8,128)(2,1)} %get-tuple-element.592, bf16[3072,1536]{1,0:T(8,128)(2,1)} %get-tuple-element.591, bf16[64,3072]{1,0:T(8,128)(2,1)S(1)} %all_gather.11, f32[64,1,3072]{2,1,0:T(1,128)S(1)} %get-tuple-element.531, ...), kind=kOutput, calls=%fused_computation.7.clone.1 | convolution fusion | flops 1210613760 | bytes 22020608 | tf_op jit(solution)/shard_map/while/body/eval_jaxpr/dot_general | solution.py:108
  694.8 25.4 %reduce-scatter.2.cloned.1.call-done = bf16[64,768]{1,0:T(8,128)(2,1)} async-done(((bf16[64,3072]{1,0:T(8,128)(2,1)}), bf16[64,768]{1,0:T(8,128)(2,1)}) %reduce-scatter.2.cloned.1.call-update) | async-done | bytes 98320 | tf_op jit(solution)/shard_map/while/body/eval_jaxpr/reduce_scatter | solution.py:111
  721.9 4.0 collective-permute-start
  728.2 55.5 %all-reduce.2.cloned.1.call-done = bf16[128,768]{1,0:T(8,128)(2,1)} async-done(((bf16[128,768]{1,0:T(8,128)(2,1)}), bf16[128,768]{1,0:T(8,128)(2,1)}) %all-reduce.2.cloned.1.call-update) | async-done | bytes 196624 | tf_op jit(solution)/shard_map/psum | solution.py:15
  786.3 3.4 all-to-all-start.1
  789.7 4.0 all-to-all-done.1
  (254 shorter events, 139.1 us)
Async XLA Ops:
  9.0 19.7 %all-to-all-start = ((bf16[32,4,768]{2,0,1:T(8,128)(2,1)}), bf16[32,4,768]{2,0,1:T(8,128)(2,1)S(1)}, u32[]{:S(2)}, u32[]{:S(2)}) async-start(bf16[32,4,768]{2,0,1:T(8,128)(2,1)} %bitcast.60), calls=%async_computation.1 | async-start | bytes 393216 | tf_op jit(solution)/shard_map/all_to_all | solution.py:68
  15.6 9.1 %copy-start = (f32[1,16,3,3072]{3,1,2,0:T(8,128)S(1)}, f32[1,16,3,3072]{3,1,2,0:T(8,128)}, u32[]{:S(2)}) copy-start(f32[1,16,3,3072]{3,1,2,0:T(8,128)} %param.16) | copy-start | bytes 1769476
  15.6 10.6 %copy-start.1 = (bf16[1,128,4,256]{3,2,1,0:T(4,128)(2,1)S(1)}, bf16[1,128,4,256]{3,2,1,0:T(4,128)(2,1)}, u32[]{:S(2)}) copy-start(bf16[1,128,4,256]{3,2,1,0:T(4,128)(2,1)} %param.21) | copy-start | bytes 786436
  15.6 15.3 %copy-start.2 = (s32[2]{0:T(128)S(1)}, s32[2]{0:T(128)}, u32[]{:S(2)}) copy-start(s32[2]{0:T(128)} %param.15) | copy-start | bytes 28
  30.9 71.1 %reduce-scatter.2.cloned.1.call-start = ((), (), s32[]{:S(2)}) async-start(), calls=%async_computation.4 | async-start | bytes 491520 | tf_op jit(solution)/shard_map/while/body/eval_jaxpr/reduce_scatter | solution.py:111
  103.6 5.6 collective-permute-start
  109.2 70.0 %reduce-scatter.2.cloned.1.call-start = ((), (), s32[]{:S(2)}) async-start(), calls=%async_computation.4 | async-start | bytes 491520 | tf_op jit(solution)/shard_map/while/body/eval_jaxpr/reduce_scatter | solution.py:111
  180.9 5.6 collective-permute-start
  186.5 70.1 %reduce-scatter.2.cloned.1.call-start = ((), (), s32[]{:S(2)}) async-start(), calls=%async_computation.4 | async-start | bytes 491520 | tf_op jit(solution)/shard_map/while/body/eval_jaxpr/reduce_scatter | solution.py:111
  258.2 5.6 collective-permute-start
  263.8 70.1 %reduce-scatter.2.cloned.1.call-start = ((), (), s32[]{:S(2)}) async-start(), calls=%async_computation.4 | async-start | bytes 491520 | tf_op jit(solution)/shard_map/while/body/eval_jaxpr/reduce_scatter | solution.py:111
  335.5 5.6 collective-permute-start
  341.1 70.1 %reduce-scatter.2.cloned.1.call-start = ((), (), s32[]{:S(2)}) async-start(), calls=%async_computation.4 | async-start | bytes 491520 | tf_op jit(solution)/shard_map/while/body/eval_jaxpr/reduce_scatter | solution.py:111
  412.8 5.6 collective-permute-start
  418.4 70.1 %reduce-scatter.2.cloned.1.call-start = ((), (), s32[]{:S(2)}) async-start(), calls=%async_computation.4 | async-start | bytes 491520 | tf_op jit(solution)/shard_map/while/body/eval_jaxpr/reduce_scatter | solution.py:111
  490.1 5.6 collective-permute-start
  495.6 70.1 %reduce-scatter.2.cloned.1.call-start = ((), (), s32[]{:S(2)}) async-start(), calls=%async_computation.4 | async-start | bytes 491520 | tf_op jit(solution)/shard_map/while/body/eval_jaxpr/reduce_scatter | solution.py:111
  567.3 5.6 collective-permute-start
  573.0 70.0 %reduce-scatter.2.cloned.1.call-start = ((), (), s32[]{:S(2)}) async-start(), calls=%async_computation.4 | async-start | bytes 491520 | tf_op jit(solution)/shard_map/while/body/eval_jaxpr/reduce_scatter | solution.py:111
  644.6 5.6 collective-permute-start
  650.2 70.0 %reduce-scatter.2.cloned.1.call-start = ((), (), s32[]{:S(2)}) async-start(), calls=%async_computation.4 | async-start | bytes 491520 | tf_op jit(solution)/shard_map/while/body/eval_jaxpr/reduce_scatter | solution.py:111
  721.9 5.6 collective-permute-start
  727.5 56.3 %all-reduce.2.cloned.1.call-start = ((), (), s32[]{:S(2)}) async-start(), calls=%async_computation.3 | async-start | bytes 393216 | tf_op jit(solution)/shard_map/psum | solution.py:15
  786.3 7.4 all-to-all-start.1
Sparse Core Ops, SparseCore 0:
  74.7 27.3 reduce-scatter.1
  153.0 26.2 reduce-scatter.1
  230.3 26.2 reduce-scatter.1
  307.5 26.2 reduce-scatter.1
  384.8 26.2 reduce-scatter.1
  462.1 26.2 reduce-scatter.1
  539.4 26.2 reduce-scatter.1
  616.7 26.2 reduce-scatter.1
  694.0 26.2 reduce-scatter.1
Sparse Core Ops, SparseCore 1:
  730.2 53.5 all-reduce.1
where the time goes:
time: 808 us; the launch traced here: 802 us
  waiting for transfers between devices  303 us (38%)
  matrix products  194 us (24%)
  local copies, waits for them, and re-layouts  131 us (16%)
  blocking collectives  76 us (9%)
  starting transfers between devices  43.4 us (5%)
  other arithmetic  32.3 us (4%)
  between operations  14.6 us (2%)
    reduce_scatter x9, waiting for transfers between devices, work(): lax.psum_scatter(partial_value.astype(jnp.bfloat16), 'req', scatter_dimen...  230 us
    dot_general x9, matrix products, work(): jnp.dot(mlp_act, mlp_out_weight, preferred_element_type=jnp.float32)  95.7 us
    all_gather x9, blocking collectives, work(): current = lax.all_gather(incoming, 'req', axis=1, tiled=True)  76 us
    slice x9, local copies, waits for them, and re-layouts, work(): mod_rows[:, 2]  65.2 us
    psum x1, waiting for transfers between devices, spread_2(): return lax.psum(kept, axis)  55.5 us
    dot_general x9, matrix products, work(): jnp.dot(normed, qkv_weight, preferred_element_type=jnp.float32)  49.6 us
    ppermute x9, starting transfers between devices, from_behind(): return lax.ppermute(block, axis, route)  35.7 us
    reshape x9, local copies, waits for them, and re-layouts, work(): jnp.dot(onehot, mod_table, precision=lax.Precision.HIGHEST)  28.1 us
  transfers between devices with their start and end apart: 21, of which 20 were waited for; matrix products, arithmetic and copies ran while one was open for 3% of the time, Pallas kernels for 0%

commit v1 on v0

--- a/solution.py
+++ b/solution.py
@@ -1,6 +1,10 @@
+import functools
+
 import jax
 import jax.numpy as jnp
 from jax import lax
+from jax.experimental import pallas as pl
+from jax.experimental.pallas import tpu as pltpu
 from jax.sharding import PartitionSpec as P
 
 
@@ -30,7 +34,7 @@
     )
 
 
-def shards(
+def plain_shards(
     latents,
     patch_route,
     request_len,
@@ -149,6 +153,408 @@
     return lax.dynamic_slice_in_dim(owned, section_index * section_cols, section_cols, 1)
 
 
+MESH = pl.DeviceIdType.MESH
+F32 = jnp.float32
+BF16 = jnp.bfloat16
+
+
+def dot(left, right, dims=((1,), (0,)), precision=None):
+    return lax.dot_general(
+        left, right, (dims, ((), ())), precision=precision, preferred_element_type=F32
+    )
+
+
+def relay_kernel(
+    sections,
+    reqs,
+    route_ref,
+    len_ref,
+    order_ref,
+    latents_ref,
+    mod_ref,
+    stale_ref,
+    w_qkv_ref,
+    w_in_ref,
+    w_attn_ref,
+    w_mlp_ref,
+    out_ref,
+    wq,
+    wi,
+    wo,
+    lat,
+    xin,
+    normed,
+    act,
+    kv,
+    same,
+    perm,
+    mods,
+    part_send,
+    part_recv,
+    xnew,
+    xfin,
+    fin_send,
+    fin_recv,
+    w_sem,
+    lat_ssem,
+    lat_rsem,
+    x_ssem,
+    x_rsem,
+    p_ssem,
+    p_rsem,
+    f_ssem,
+    f_rsem,
+):
+    s = lax.axis_index("section")
+    r = lax.axis_index("req")
+    devices = sections * reqs
+    per = sections // reqs
+    patches, width = lat.shape
+    rows = patches // 2
+    cols = width // reqs
+    own_rows = patches // reqs
+    heads, _, head_width = wq.shape
+    hd = head_width // 3
+    attn_width = heads * hd
+    mlp_width = wi.shape[1]
+    req_total = mod_ref.shape[1]
+
+    loads = [
+        pltpu.make_async_copy(w_qkv_ref, wq, w_sem.at[0]),
+        pltpu.make_async_copy(w_in_ref, wi, w_sem.at[1]),
+        pltpu.make_async_copy(w_attn_ref, wo.at[pl.ds(0, attn_width)], w_sem.at[2]),
+        pltpu.make_async_copy(w_mlp_ref, wo.at[pl.ds(attn_width, mlp_width)], w_sem.at[3]),
+    ]
+    for load in loads:
+        load.start()
+
+    barrier = pltpu.get_barrier_semaphore()
+    me = s * reqs + r
+
+    def greet(step, carry):
+        target = lax.rem(me + step, devices)
+        pl.semaphore_signal(
+            barrier,
+            inc=1,
+            device_id=(lax.div(target, reqs), lax.rem(target, reqs)),
+            device_id_type=MESH,
+        )
+        return carry
+
+    lax.fori_loop(1, devices, greet, 0)
+    pl.semaphore_wait(barrier, devices - 1)
+
+    def peer(step):
+        return lax.rem(r + step, reqs)
+
+    def lat_copy(step):
+        mine = lat.at[pl.ds(pl.multiple_of(r * own_rows, own_rows), own_rows)]
+        return pltpu.make_async_remote_copy(
+            src_ref=latents_ref,
+            dst_ref=mine,
+            send_sem=lat_ssem.at[step],
+            recv_sem=lat_rsem.at[step],
+            device_id=(s, peer(step)),
+            device_id_type=MESH,
+        )
+
+    @pl.when(s == 0)
+    def _():
+        for step in range(1, reqs):
+            lat_copy(step).start()
+        lat[pl.ds(pl.multiple_of(r * own_rows, own_rows), own_rows), :] = latents_ref[...]
+
+    place = lax.broadcasted_iota(jnp.int32, (patches, patches), 0)
+    lane = lax.broadcasted_iota(jnp.int32, (patches, patches), 1)
+    first, second = order_ref[0], order_ref[1]
+    position = jnp.where(place < rows, first * rows + place, second * rows + place - rows)
+    chosen = lane == position
+    route = jnp.sum(
+        jnp.where(chosen, jnp.broadcast_to(route_ref[...], chosen.shape), 0).astype(F32),
+        axis=1,
+        keepdims=True,
+    )
+    perm[...] = (lane.astype(F32) == route).astype(BF16)
+    req_lane = lax.broadcasted_iota(jnp.int32, (patches, req_total), 1)
+    owner = jnp.zeros((patches, req_total), F32)
+    start = jnp.int32(0)
+    for q in range(req_total):
+        end = start + len_ref[q]
+        inside = (route >= start.astype(F32)) & (route < end.astype(F32))
+        owner = jnp.where((req_lane == q) & inside, 1.0, owner)
+        start = end
+    same[...] = dot(owner, owner, ((1,), (1,)))
+    chosen_bf = chosen.astype(F32).astype(BF16)
+    for h in range(heads):
+        kv[h, rows:, :] = dot(chosen_bf[rows:, :], stale_ref[h]).astype(BF16)
+    for k in range(3):
+        for c in range(reqs):
+            at = pl.ds(c * cols, cols)
+            value = dot(owner, mod_ref[k, :, at], precision=lax.Precision.HIGHEST)
+            mods[k, :, at] = value + 1.0 if k == 1 else value
+
+    @pl.when(s == 0)
+    def _():
+        for step in range(1, reqs):
+            lat_copy(step).wait_recv()
+        for c in range(reqs):
+            entry = dot(perm[...], lat[:, c * cols : (c + 1) * cols]).astype(BF16)
+            xin[0, c] = entry[:rows]
+            xin[1, c] = entry[rows:]
+
+    def x_copy(t, q, source):
+        return pltpu.make_async_remote_copy(
+            src_ref=xnew.at[t],
+            dst_ref=xin.at[t, source],
+            send_sem=x_ssem.at[t, q],
+            recv_sem=x_rsem.at[t, source],
+            device_id=(lax.rem(s + 1, sections), q),
+            device_id_type=MESH,
+        )
+
+    def part_copy(t, step):
+        return pltpu.make_async_remote_copy(
+            src_ref=part_send.at[t, step],
+            dst_ref=part_recv.at[t, step],
+            send_sem=p_ssem.at[t, step],
+            recv_sem=p_rsem.at[t, step],
+            device_id=(s, peer(step)),
+            device_id_type=MESH,
+        )
+
+    def slot(t, carry):
+        at_rows = pl.ds(pl.multiple_of(t * rows, rows), rows)
+
+        @pl.when(s > 0)
+        def _():
+            for q in range(reqs):
+                x_copy(t, q, q).wait_recv()
+
+        total = jnp.zeros((rows, 1), F32)
+        for c in range(reqs):
+            total = total + jnp.sum(xin[t, c].astype(F32), axis=1, keepdims=True)
+        mean = total / width
+        square = jnp.zeros((rows, 1), F32)
+        for c in range(reqs):
+            centered = xin[t, c].astype(F32) - mean
+            square = square + jnp.sum(centered * centered, axis=1, keepdims=True)
+        scale = lax.rsqrt(square / width + 1e-06)
+        for c in range(reqs):
+            at = pl.ds(c * cols, cols)
+            value = (xin[t, c].astype(F32) - mean) * scale
+            normed[:, at] = (value * mods[1, at_rows, at] + mods[0, at_rows, at]).astype(BF16)
+
+        @pl.when(t == 0)
+        def _():
+            loads[0].wait()
+
+        allowed = same[at_rows, :] > 0.5
+        for h in range(heads):
+            qkv = dot(normed[...], wq[h])
+            kv[h, at_rows, :] = qkv[:, hd:].astype(BF16)
+            scores = dot(qkv[:, :hd].astype(BF16), kv[h, :, :hd], ((1,), (1,))) * (hd**-0.5)
+            scores = jnp.where(allowed, scores, -jnp.inf)
+            top = jnp.max(scores, axis=1, keepdims=True)
+            weights = jnp.exp(scores - top)
+            weights = weights / jnp.sum(weights, axis=1, keepdims=True)
+            act[:, h * hd : (h + 1) * hd] = dot(weights.astype(BF16), kv[h, :, hd:]).astype(BF16)
+
+        @pl.when(t == 0)
+        def _():
+            loads[1].wait()
+
+        piece = mlp_width // 3 if mlp_width % 384 == 0 else mlp_width
+        for c in range(mlp_width // piece):
+            hidden = dot(normed[...], wi[:, c * piece : (c + 1) * piece])
+            act[:, attn_width + c * piece : attn_width + (c + 1) * piece] = gelu_tanh(
+                hidden
+            ).astype(BF16)
+
+        @pl.when(t == 0)
+        def _():
+            loads[2].wait()
+            loads[3].wait()
+
+        for step in [*range(reqs - 1, 0, -1), 0]:
+            at = pl.ds(pl.multiple_of(peer(step) * cols, cols), cols)
+            part_send[t, step] = dot(act[...], wo[:, at]).astype(BF16)
+            if step > 0:
+                part_copy(t, step).start()
+        branch = part_send[t, 0].astype(F32)
+        for step in range(reqs - 1, 0, -1):
+            part_copy(t, step).wait_recv()
+            branch = branch + part_recv[t, step].astype(F32)
+        own = pl.ds(pl.multiple_of(r * cols, cols), cols)
+        gated = mods[2, at_rows, own] * branch
+        updated = (xin[t, r].astype(F32) + gated).astype(BF16)
+        xnew[t] = updated
+
+        @pl.when(s < sections - 1)
+        def _():
+            for q in range(reqs):
+                x_copy(t, q, r).start()
+
+        @pl.when(s == sections - 1)
+        def _():
+            xfin[at_rows, :] = updated
+
+        return carry
+
+    lax.fori_loop(0, 2, slot, 0)
+
+    last_own = (sections - 1) // per
+    is_self = (s == sections - 1) & (r == last_own)
+
+    def fin_copy(u, q):
+        return pltpu.make_async_remote_copy(
+            src_ref=fin_send.at[u, q],
+            dst_ref=fin_recv,
+            send_sem=f_ssem.at[u, q],
+            recv_sem=f_rsem.at[0],
+            device_id=(r * per + u, q),
+            device_id_type=MESH,
+        )
+
+    def to_self(u, q):
+        return (r * per + u == sections - 1) & (r == q)
+
+    @pl.when(s == sections - 1)
+    def _():
+        done = dot(perm[...], xfin[...], ((0,), (0,))).astype(BF16)
+        out_cols = cols // per
+        for u in range(per):
+            for q in range(reqs):
+                block = done[q * own_rows : (q + 1) * own_rows, u * out_cols : (u + 1) * out_cols]
+                fin_send[u, q] = block
+
+                @pl.when(to_self(u, q))
+                def _():
+                    out_ref[...] = block
+
+                @pl.when(jnp.logical_not(to_self(u, q)))
+                def _():
+                    fin_copy(u, q).start()
+
+    @pl.when(jnp.logical_not(is_self))
+    def _():
+        fin_copy(0, 0).wait_recv()
+        out_ref[...] = fin_recv[...]
+
+    @pl.when(s == sections - 1)
+    def _():
+        for u in range(per):
+            for q in range(reqs):
+
+                @pl.when(jnp.logical_not(to_self(u, q)))
+                def _():
+                    fin_copy(u, q).wait_send()
+
+    @pl.when(s == 0)
+    def _():
+        for step in range(1, reqs):
+            lat_copy(step).wait_send()
+
+    for t in range(2):
+        for step in range(1, reqs):
+            part_copy(t, step).wait_send()
+
+    @pl.when(s < sections - 1)
+    def _():
+        for t in range(2):
+            for q in range(reqs):
+                x_copy(t, q, r).wait_send()
+
+
+def relay_shards(
+    latents,
+    patch_route,
+    request_len,
+    span_order,
+    modulation,
+    w_qkv,
+    w_mlp_in,
+    w_out_attn,
+    w_out_mlp,
+    stale_kv,
+):
+    sections = lax.axis_size("section")
+    reqs = lax.axis_size("req")
+    patches = patch_route.shape[0]
+    own_rows, width = latents.shape
+    heads, head_width = w_qkv.shape[2:]
+    hd = head_width // 3
+    mlp_width = w_mlp_in.shape[2]
+    rows, cols, per = patches // 2, width // reqs, sections // reqs
+    out_cols = width // sections
+    vmem = pl.BlockSpec(memory_space=pltpu.VMEM)
+    smem = pl.BlockSpec(memory_space=pltpu.SMEM)
+    hbm = pl.BlockSpec(memory_space=pl.ANY)
+    weights = width * (heads * head_width + mlp_width) + (heads * hd + mlp_width) * width
+    return pl.pallas_call(
+        functools.partial(relay_kernel, sections, reqs),
+        out_shape=jax.ShapeDtypeStruct((own_rows, out_cols), BF16),
+        in_specs=[vmem, smem, smem, vmem, vmem, vmem, hbm, hbm, hbm, hbm],
+        out_specs=vmem,
+        scratch_shapes=[
+            pltpu.VMEM((heads, width, head_width), BF16),
+            pltpu.VMEM((width, mlp_width), BF16),
+            pltpu.VMEM((heads * hd + mlp_width, width), BF16),
+            pltpu.VMEM((patches, width), BF16),
+            pltpu.VMEM((2, reqs, rows, cols), BF16),
+            pltpu.VMEM((rows, width), BF16),
+            pltpu.VMEM((rows, heads * hd + mlp_width), BF16),
+            pltpu.VMEM((heads, patches, 2 * hd), BF16),
+            pltpu.VMEM((patches, patches), F32),
+            pltpu.VMEM((patches, patches), BF16),
+            pltpu.VMEM((3, patches, width), F32),
+            pltpu.VMEM((2, reqs, rows, cols), BF16),
+            pltpu.VMEM((2, reqs, rows, cols), BF16),
+            pltpu.VMEM((2, rows, cols), BF16),
+            pltpu.VMEM((patches, cols), BF16),
+            pltpu.VMEM((per, reqs, own_rows, out_cols), BF16),
+            pltpu.VMEM((own_rows, out_cols), BF16),
+            pltpu.SemaphoreType.DMA((4,)),
+            pltpu.SemaphoreType.DMA((reqs,)),
+            pltpu.SemaphoreType.DMA((reqs,)),
+            pltpu.SemaphoreType.DMA((2, reqs)),
+            pltpu.SemaphoreType.DMA((2, reqs)),
+            pltpu.SemaphoreType.DMA((2, reqs)),
+            pltpu.SemaphoreType.DMA((2, reqs)),
+            pltpu.SemaphoreType.DMA((per, reqs)),
+            pltpu.SemaphoreType.DMA((1,)),
+        ],
+        compiler_params=pltpu.CompilerParams(
+            collective_id=0, has_side_effects=True, vmem_limit_bytes=58 * 2**20
+        ),
+        cost_estimate=pl.CostEstimate(
+            flops=2 * patches * weights, bytes_accessed=2 * weights, transcendentals=0
+        ),
+    )(
+        patch_route.reshape(1, patches),
+        request_len,
+        span_order,
+        latents,
+        jnp.transpose(modulation[0], (1, 0, 2)),
+        jnp.transpose(stale_kv[0], (1, 0, 2)),
+        jnp.transpose(w_qkv[0], (1, 0, 2)),
+        w_mlp_in[0],
+        w_out_attn[0].reshape(heads * hd, width),
+        w_out_mlp[0],
+    )
+
+
+def shards(*arrays):
+    sections, reqs = lax.axis_size("section"), lax.axis_size("req")
+    width, patches = arrays[0].shape[1], arrays[1].shape[0]
+    fits = (
+        arrays[3].shape[0] == 2
+        and sections % reqs == 0
+        and width % (sections * 128) == 0
+        and patches % (reqs * 16) == 0
+    )
+    return (relay_shards if fits else plain_shards)(*arrays)
+
+
 def solution(mesh):
     in_specs = (
         P("req", None),

time: 808 us -> 187 us (0.23)
  waiting for transfers between devices: 303 us -> 0 us
  matrix products: 194 us -> 0 us
  Pallas kernels: 0 us -> 175 us
  local copies, waits for them, and re-layouts: 131 us -> 11.5 us
  blocking collectives: 76 us -> 0 us
  starting transfers between devices: 43.4 us -> 0 us
  other arithmetic: 32.3 us -> 0 us
  between operations: 14.6 us -> 0.01 us
    reduce_scatter x9 -> x0, waiting for transfers between devices: 230 us -> none  [work(): lax.psum_scatter(partial_value.astype(jnp.bfloat16), 'req', scatter_dimen...]
    dot_general x54 -> x0, matrix products: 194 us -> none  [the longest x9 95.7 us: work(): jnp.dot(mlp_act, mlp_out_weight, preferred_element_type=jnp.float32)]
    pallas_call x0 -> x1, Pallas kernels: none -> 175 us  [relay_shards(): pl.pallas_call(functools.partial(relay_kernel, sections, reqs), out_shape...]
    all_gather x9 -> x0, blocking collectives: 76 us -> none  [work(): current = lax.all_gather(incoming, 'req', axis=1, tiled=True)]
    slice x27 -> x0, local copies, waits for them, and re-layouts: 65.9 us -> none  [the longest x9 65.2 us: work(): mod_rows[:, 2]]
    psum x1 -> x0, waiting for transfers between devices: 55.5 us -> none  [spread_2(): return lax.psum(kept, axis)]
    ppermute x9 -> x0, starting transfers between devices: 35.7 us -> none  [from_behind(): return lax.ppermute(block, axis, route)]
    reshape x9 -> x0, local copies, waits for them, and re-layouts: 28.1 us -> none  [work(): jnp.dot(onehot, mod_table, precision=lax.Precision.HIGHEST)]
  transfers between devices with their start and end apart: 21 -> 0, of which waited for: 20 -> 0; matrix products, arithmetic and copies ran while one was open for 3% -> 0% of each run, Pallas kernels for 0% -> 0%
where the time goes in v1:
time: 187 us; the launch traced here: 186 us
  Pallas kernels  175 us (94%)
  local copies, waits for them, and re-layouts  11.5 us (6%)
    pallas_call x1, Pallas kernels, relay_shards(): pl.pallas_call(functools.partial(relay_kernel, sections, reqs), out_shape...  175 us
    unnamed x3, local copies, waits for them, and re-layouts  11.5 us

profile of v1, /device:TPU:1, one launch (start us, length us, event | category | flops | bytes accessed | tf_op | source)
XLA Modules:
  0.0 186.4 jit_solution(5114620015704616056)
XLA Ops:
  0.0 1.7 copy.16
  1.7 8.5 %copy.15 = bf16[1,3072,4,384]{3,1,2,0:T(8,128)(2,1)} copy(bf16[1,3072,4,384]{3,2,1,0:T(4,128)(2,1)} %param.15) | data formatting | bytes 18874368 | tf_op args[5]
  10.2 174.8 %shard_map.100 = bf16[32,384]{1,0:T(8,128)(2,1)} custom-call(s32[1,128]{1,0:T(1,128)} %bitcast.23, s32[16]{0:T(128)} %len_ref.1, s32[2]{0:T(128)} %order_ref.1, bf16[32,3072]{1,0:T(8,128)(2,1)} %latents_ref.1, f32[3,16,3072]{2,1,0:T(8,128)} %bitcast.22, bf16[4,128,256]{2,1,0:T(8,128)(2,1)} %bitcast.21, bf16[4,3072,384]{2,1,0:T(8,128)(2,1)} %bitcast.17, ...), custom_call_target="tpu_custom_call" | custom-call | flops 4026531840 | bytes 31457280 | tf_op jit(solution)/shard_map/pallas_call | solution.py:493
  185.0 1.3 copy.18

commit v2 on v1

--- a/solution.py
+++ b/solution.py
@@ -213,19 +213,25 @@
     rows = patches // 2
     cols = width // reqs
     own_rows = patches // reqs
-    heads, _, head_width = wq.shape
+    heads, _, head_width = w_qkv_ref.shape
     hd = head_width // 3
+    pieces = [(0, cols)] if cols < 512 else [(0, cols - 256), (cols - 256, 256)]
     attn_width = heads * hd
     mlp_width = wi.shape[1]
     req_total = mod_ref.shape[1]
 
     loads = [
-        pltpu.make_async_copy(w_qkv_ref, wq, w_sem.at[0]),
-        pltpu.make_async_copy(w_in_ref, wi, w_sem.at[1]),
-        pltpu.make_async_copy(w_attn_ref, wo.at[pl.ds(0, attn_width)], w_sem.at[2]),
-        pltpu.make_async_copy(w_mlp_ref, wo.at[pl.ds(attn_width, mlp_width)], w_sem.at[3]),
+        pltpu.make_async_copy(
+            w_qkv_ref.at[h], wq.at[:, pl.ds(h * head_width, head_width)], w_sem.at[3 + h]
+        )
+        for h in range(heads)
     ]
-    for load in loads:
+    loads.append(pltpu.make_async_copy(w_in_ref, wi, w_sem.at[0]))
+    late_loads = [
+        pltpu.make_async_copy(w_attn_ref, wo.at[pl.ds(0, attn_width)], w_sem.at[1]),
+        pltpu.make_async_copy(w_mlp_ref, wo.at[pl.ds(attn_width, mlp_width)], w_sem.at[2]),
+    ]
+    for load in loads + late_loads:
         load.start()
 
     barrier = pltpu.get_barrier_semaphore()
@@ -245,7 +251,10 @@
     pl.semaphore_wait(barrier, devices - 1)
 
     def peer(step):
-        return lax.rem(r + step, reqs)
+        if reqs % 2:
+            return lax.rem(r + step, reqs)
+        across = lax.rem(lax.div(r, 2) + step // 2, reqs // 2)
+        return across * 2 + lax.rem(r + step, 2)
 
     def lat_copy(step):
         mine = lat.at[pl.ds(pl.multiple_of(r * own_rows, own_rows), own_rows)]
@@ -302,22 +311,24 @@
             xin[0, c] = entry[:rows]
             xin[1, c] = entry[rows:]
 
-    def x_copy(t, q, source):
+    def x_copy(p, t, q, source):
+        at = pl.ds(*pieces[p])
         return pltpu.make_async_remote_copy(
-            src_ref=xnew.at[t],
-            dst_ref=xin.at[t, source],
-            send_sem=x_ssem.at[t, q],
-            recv_sem=x_rsem.at[t, source],
+            src_ref=xnew.at[t, :, at],
+            dst_ref=xin.at[t, source, :, at],
+            send_sem=x_ssem.at[p, t, q],
+            recv_sem=x_rsem.at[p, t, source],
             device_id=(lax.rem(s + 1, sections), q),
             device_id_type=MESH,
         )
 
-    def part_copy(t, step):
+    def part_copy(p, t, step):
+        at = pl.ds(*pieces[p])
         return pltpu.make_async_remote_copy(
-            src_ref=part_send.at[t, step],
-            dst_ref=part_recv.at[t, step],
-            send_sem=p_ssem.at[t, step],
-            recv_sem=p_rsem.at[t, step],
+            src_ref=part_send.at[t, step, :, at],
+            dst_ref=part_recv.at[t, step, :, at],
+            send_sem=p_ssem.at[p, t, step],
+            recv_sem=p_rsem.at[p, t, step],
             device_id=(s, peer(step)),
             device_id_type=MESH,
         )
@@ -325,19 +336,21 @@
     def slot(t, carry):
         at_rows = pl.ds(pl.multiple_of(t * rows, rows), rows)
 
-        @pl.when(s > 0)
-        def _():
+        stats = []
+        for p, (begin, size) in enumerate(pieces):
             for q in range(reqs):
-                x_copy(t, q, q).wait_recv()
-
-        total = jnp.zeros((rows, 1), F32)
-        for c in range(reqs):
-            total = total + jnp.sum(xin[t, c].astype(F32), axis=1, keepdims=True)
-        mean = total / width
-        square = jnp.zeros((rows, 1), F32)
-        for c in range(reqs):
-            centered = xin[t, c].astype(F32) - mean
-            square = square + jnp.sum(centered * centered, axis=1, keepdims=True)
+
+                @pl.when(s > 0)
+                def _():
+                    x_copy(p, t, q, q).wait_recv()
+
+            for q in range(reqs):
+                value = xin[t, q, :, begin : begin + size].astype(F32)
+                mean = jnp.sum(value, axis=1, keepdims=True) / size
+                value = value - mean
+                stats.append((size, mean, jnp.sum(value * value, axis=1, keepdims=True)))
+        mean = sum(size * part for size, part, _ in stats) / width
+        square = sum(part + size * (at - mean) * (at - mean) for size, at, part in stats)
         scale = lax.rsqrt(square / width + 1e-06)
         for c in range(reqs):
             at = pl.ds(c * cols, cols)
@@ -346,57 +359,81 @@
 
         @pl.when(t == 0)
         def _():
-            loads[0].wait()
+            for load in loads:
+                load.wait()
 
         allowed = same[at_rows, :] > 0.5
+        group = 2 if heads % 2 == 0 else 1
+        queries = []
+        for g in range(heads // group):
+            span = group * head_width
+            qkv = dot(normed[...], wq[:, g * span : (g + 1) * span])
+            for h in range(group):
+                begin = h * head_width
+                queries.append(qkv[:, begin : begin + hd].astype(BF16))
+                fresh = qkv[:, begin + hd : begin + head_width].astype(BF16)
+                kv[g * group + h, at_rows, :] = fresh
+
+        piece = mlp_width // 3 if mlp_width % 384 == 0 else mlp_width
+        chunks = mlp_width // piece
+
+        def up(c):
+            return dot(normed[...], wi[:, c * piece : (c + 1) * piece])
+
+        def keep(c, hidden):
+            at = attn_width + c * piece
+            act[:, at : at + piece] = gelu_tanh(hidden).astype(BF16)
+
+        scores = [dot(queries[h], kv[h, :, :hd], ((1,), (1,))) for h in range(heads)]
+        hidden = up(0)
+        attention = []
         for h in range(heads):
-            qkv = dot(normed[...], wq[h])
-            kv[h, at_rows, :] = qkv[:, hd:].astype(BF16)
-            scores = dot(qkv[:, :hd].astype(BF16), kv[h, :, :hd], ((1,), (1,))) * (hd**-0.5)
-            scores = jnp.where(allowed, scores, -jnp.inf)
-            top = jnp.max(scores, axis=1, keepdims=True)
-            weights = jnp.exp(scores - top)
+            score = jnp.where(allowed, scores[h] * (hd**-0.5), -jnp.inf)
+            top = jnp.max(score, axis=1, keepdims=True)
+            weights = jnp.exp(score - top)
             weights = weights / jnp.sum(weights, axis=1, keepdims=True)
-            act[:, h * hd : (h + 1) * hd] = dot(weights.astype(BF16), kv[h, :, hd:]).astype(BF16)
+            attention.append(weights.astype(BF16))
+        keep(0, hidden)
+        for c in range(1, chunks):
+            hidden = up(c)
+            if c == 1:
+                for h in range(heads):
+                    act[:, h * hd : (h + 1) * hd] = dot(attention[h], kv[h, :, hd:]).astype(BF16)
+            keep(c, hidden)
+        if chunks == 1:
+            for h in range(heads):
+                act[:, h * hd : (h + 1) * hd] = dot(attention[h], kv[h, :, hd:]).astype(BF16)
 
         @pl.when(t == 0)
         def _():
-            loads[1].wait()
-
-        piece = mlp_width // 3 if mlp_width % 384 == 0 else mlp_width
-        for c in range(mlp_width // piece):
-            hidden = dot(normed[...], wi[:, c * piece : (c + 1) * piece])
-            act[:, attn_width + c * piece : attn_width + (c + 1) * piece] = gelu_tanh(
-                hidden
-            ).astype(BF16)
-
-        @pl.when(t == 0)
-        def _():
-            loads[2].wait()
-            loads[3].wait()
-
-        for step in [*range(reqs - 1, 0, -1), 0]:
-            at = pl.ds(pl.multiple_of(peer(step) * cols, cols), cols)
-            part_send[t, step] = dot(act[...], wo[:, at]).astype(BF16)
-            if step > 0:
-                part_copy(t, step).start()
-        branch = part_send[t, 0].astype(F32)
-        for step in range(reqs - 1, 0, -1):
-            part_copy(t, step).wait_recv()
-            branch = branch + part_recv[t, step].astype(F32)
-        own = pl.ds(pl.multiple_of(r * cols, cols), cols)
-        gated = mods[2, at_rows, own] * branch
-        updated = (xin[t, r].astype(F32) + gated).astype(BF16)
-        xnew[t] = updated
-
-        @pl.when(s < sections - 1)
-        def _():
-            for q in range(reqs):
-                x_copy(t, q, r).start()
+            for load in late_loads:
+                load.wait()
+
+        for p, (begin, size) in enumerate(pieces):
+            for step in [*range(reqs - 1, 0, -1), 0]:
+                at = pl.ds(pl.multiple_of(peer(step) * cols + begin, 128), size)
+                product = dot(act[...], wo[:, at]).astype(BF16)
+                part_send[t, step, :, begin : begin + size] = product
+                if step > 0:
+                    part_copy(p, t, step).start()
+        for p, (begin, size) in enumerate(pieces):
+            branch = part_send[t, 0, :, begin : begin + size].astype(F32)
+            for step in range(1, reqs):
+                part_copy(p, t, step).wait_recv()
+                branch = branch + part_recv[t, step, :, begin : begin + size].astype(F32)
+            own = pl.ds(pl.multiple_of(r * cols + begin, 128), size)
+            gated = mods[2, at_rows, own] * branch
+            updated = xin[t, r, :, begin : begin + size].astype(F32) + gated
+            xnew[t, :, begin : begin + size] = updated.astype(BF16)
+
+            @pl.when(s < sections - 1)
+            def _():
+                for step in range(reqs - 1, -1, -1):
+                    x_copy(p, t, peer(step), r).start()
 
         @pl.when(s == sections - 1)
         def _():
-            xfin[at_rows, :] = updated
+            xfin[at_rows, :] = xnew[t]
 
         return carry
 
@@ -454,15 +491,17 @@
         for step in range(1, reqs):
             lat_copy(step).wait_send()
 
-    for t in range(2):
-        for step in range(1, reqs):
-            part_copy(t, step).wait_send()
+    for p in range(len(pieces)):
+        for t in range(2):
+            for step in range(1, reqs):
+                part_copy(p, t, step).wait_send()
 
     @pl.when(s < sections - 1)
     def _():
-        for t in range(2):
-            for q in range(reqs):
-                x_copy(t, q, r).wait_send()
+        for p in range(len(pieces)):
+            for t in range(2):
+                for q in range(reqs):
+                    x_copy(p, t, q, r).wait_send()
 
 
 def relay_shards(
@@ -496,7 +535,7 @@
         in_specs=[vmem, smem, smem, vmem, vmem, vmem, hbm, hbm, hbm, hbm],
         out_specs=vmem,
         scratch_shapes=[
-            pltpu.VMEM((heads, width, head_width), BF16),
+            pltpu.VMEM((width, heads * head_width), BF16),
             pltpu.VMEM((width, mlp_width), BF16),
             pltpu.VMEM((heads * hd + mlp_width, width), BF16),
             pltpu.VMEM((patches, width), BF16),
@@ -513,13 +552,13 @@
             pltpu.VMEM((patches, cols), BF16),
             pltpu.VMEM((per, reqs, own_rows, out_cols), BF16),
             pltpu.VMEM((own_rows, out_cols), BF16),
-            pltpu.SemaphoreType.DMA((4,)),
+            pltpu.SemaphoreType.DMA((3 + heads,)),
             pltpu.SemaphoreType.DMA((reqs,)),
             pltpu.SemaphoreType.DMA((reqs,)),
-            pltpu.SemaphoreType.DMA((2, reqs)),
-            pltpu.SemaphoreType.DMA((2, reqs)),
-            pltpu.SemaphoreType.DMA((2, reqs)),
-            pltpu.SemaphoreType.DMA((2, reqs)),
+            pltpu.SemaphoreType.DMA((2, 2, reqs)),
+            pltpu.SemaphoreType.DMA((2, 2, reqs)),
+            pltpu.SemaphoreType.DMA((2, 2, reqs)),
+            pltpu.SemaphoreType.DMA((2, 2, reqs)),
             pltpu.SemaphoreType.DMA((per, reqs)),
             pltpu.SemaphoreType.DMA((1,)),
         ],

time: 187 us -> 156 us (0.83)
  Pallas kernels: 175 us -> 144 us
    pallas_call x1, Pallas kernels: 175 us -> 144 us  [relay_shards(): pl.pallas_call(functools.partial(relay_kernel, sections, reqs), out_shape...]
where the time goes in v2:
time: 156 us
  Pallas kernels  144 us (92%)
  local copies, waits for them, and re-layouts  11.5 us (7%)
    pallas_call x1, Pallas kernels, relay_shards(): pl.pallas_call(functools.partial(relay_kernel, sections, reqs), out_shape...  144 us
    unnamed x3, local copies, waits for them, and re-layouts  11.5 us

profile of v2, /device:TPU:1, one launch (start us, length us, event | category | flops | bytes accessed | tf_op | source)
XLA Modules:
  0.0 156.0 jit_solution(4369087029058092774)
XLA Ops:
  0.0 1.7 %copy.16 = bf16[1,128,4,256]{3,1,2,0:T(8,128)(2,1)} copy(bf16[1,128,4,256]{3,2,1,0:T(4,128)(2,1)} %param.19) | data formatting | bytes 524288 | tf_op args[9]
  1.7 8.5 %copy.15 = bf16[1,3072,4,384]{3,1,2,0:T(8,128)(2,1)} copy(bf16[1,3072,4,384]{3,2,1,0:T(4,128)(2,1)} %param.15) | data formatting | bytes 18874368 | tf_op args[5]
  10.2 144.5 %shard_map.100 = bf16[32,384]{1,0:T(8,128)(2,1)} custom-call(s32[1,128]{1,0:T(1,128)} %bitcast.23, s32[16]{0:T(128)} %len_ref.1, s32[2]{0:T(128)} %order_ref.1, bf16[32,3072]{1,0:T(8,128)(2,1)} %latents_ref.1, f32[3,16,3072]{2,1,0:T(8,128)} %bitcast.22, bf16[4,128,256]{2,1,0:T(8,128)(2,1)} %bitcast.21, bf16[4,3072,384]{2,1,0:T(8,128)(2,1)} %bitcast.17, ...), custom_call_target="tpu_custom_call" | custom-call | flops 4026531840 | bytes 31457280 | tf_op jit(solution)/shard_map/pallas_call | solution.py:532
  154.7 1.3 copy.18

commit v3 on v2

--- a/solution.py
+++ b/solution.py
@@ -178,6 +178,7 @@
     w_attn_ref,
     w_mlp_ref,
     out_ref,
+    raw,
     wq,
     wi,
     wo,
@@ -213,20 +214,22 @@
     rows = patches // 2
     cols = width // reqs
     own_rows = patches // reqs
-    heads, _, head_width = w_qkv_ref.shape
+    heads, head_width = w_qkv_ref.shape[1:]
+    chunk = 256
+    chunk_count = width // chunk
     hd = head_width // 3
     pieces = [(0, cols)] if cols < 512 else [(0, cols - 256), (cols - 256, 256)]
     attn_width = heads * hd
     mlp_width = wi.shape[1]
     req_total = mod_ref.shape[1]
 
-    loads = [
-        pltpu.make_async_copy(
-            w_qkv_ref.at[h], wq.at[:, pl.ds(h * head_width, head_width)], w_sem.at[3 + h]
-        )
-        for h in range(heads)
-    ]
-    loads.append(pltpu.make_async_copy(w_in_ref, wi, w_sem.at[0]))
+    def raw_load(c):
+        at = pl.ds(pl.multiple_of(c * chunk, chunk), chunk)
+        return pltpu.make_async_copy(w_qkv_ref.at[at], raw.at[at], w_sem.at[3 + c])
+
+    for c in range(chunk_count):
+        raw_load(c).start()
+    loads = [pltpu.make_async_copy(w_in_ref, wi, w_sem.at[0])]
     late_loads = [
         pltpu.make_async_copy(w_attn_ref, wo.at[pl.ds(0, attn_width)], w_sem.at[1]),
         pltpu.make_async_copy(w_mlp_ref, wo.at[pl.ds(attn_width, mlp_width)], w_sem.at[2]),
@@ -294,13 +297,23 @@
         start = end
     same[...] = dot(owner, owner, ((1,), (1,)))
     chosen_bf = chosen.astype(F32).astype(BF16)
+    stale = stale_ref[...].reshape(patches, heads * 2 * hd)
+    stale = dot(chosen_bf[rows:, :], stale).astype(BF16)
     for h in range(heads):
-        kv[h, rows:, :] = dot(chosen_bf[rows:, :], stale_ref[h]).astype(BF16)
+        kv[h, rows:, :] = stale[:, h * 2 * hd : (h + 1) * 2 * hd]
     for k in range(3):
         for c in range(reqs):
             at = pl.ds(c * cols, cols)
             value = dot(owner, mod_ref[k, :, at], precision=lax.Precision.HIGHEST)
             mods[k, :, at] = value + 1.0 if k == 1 else value
+
+    def flatten(c, carry):
+        raw_load(c).wait()
+        at = pl.ds(pl.multiple_of(c * chunk, chunk), chunk)
+        wq[at, :] = raw[at].reshape(chunk, heads * head_width)
+        return carry
+
+    lax.fori_loop(0, chunk_count, flatten, 0)
 
     @pl.when(s == 0)
     def _():
@@ -535,6 +548,7 @@
         in_specs=[vmem, smem, smem, vmem, vmem, vmem, hbm, hbm, hbm, hbm],
         out_specs=vmem,
         scratch_shapes=[
+            pltpu.VMEM((width, heads, head_width), BF16),
             pltpu.VMEM((width, heads * head_width), BF16),
             pltpu.VMEM((width, mlp_width), BF16),
             pltpu.VMEM((heads * hd + mlp_width, width), BF16),
@@ -552,7 +566,7 @@
             pltpu.VMEM((patches, cols), BF16),
             pltpu.VMEM((per, reqs, own_rows, out_cols), BF16),
             pltpu.VMEM((own_rows, out_cols), BF16),
-            pltpu.SemaphoreType.DMA((3 + heads,)),
+            pltpu.SemaphoreType.DMA((3 + width // 256,)),
             pltpu.SemaphoreType.DMA((reqs,)),
             pltpu.SemaphoreType.DMA((reqs,)),
             pltpu.SemaphoreType.DMA((2, 2, reqs)),
@@ -574,8 +588,8 @@
         span_order,
         latents,
         jnp.transpose(modulation[0], (1, 0, 2)),
-        jnp.transpose(stale_kv[0], (1, 0, 2)),
-        jnp.transpose(w_qkv[0], (1, 0, 2)),
+        stale_kv[0],
+        w_qkv[0],
         w_mlp_in[0],
         w_out_attn[0].reshape(heads * hd, width),
         w_out_mlp[0],

time: 156 us -> 147 us (0.942)
  local copies, waits for them, and re-layouts: 11.5 us -> 1.35 us
    unnamed x3 -> x1, local copies, waits for them, and re-layouts: 11.5 us -> 1.35 us
where the time goes in v3:
time: 147 us; the launch traced here: 146 us
  Pallas kernels  145 us (99%)
    pallas_call x1, Pallas kernels, relay_shards(): pl.pallas_call(functools.partial(relay_kernel, sections, reqs), out_shape...  145 us

profile of v3, /device:TPU:1, one launch (start us, length us, event | category | flops | bytes accessed | tf_op | source)
XLA Modules:
  0.0 146.3 jit_solution(8361946439734468304)
XLA Ops:
  0.0 145.0 %shard_map.100 = bf16[32,384]{1,0:T(8,128)(2,1)} custom-call(s32[1,128]{1,0:T(1,128)} %bitcast.15, s32[16]{0:T(128)} %len_ref.1, s32[2]{0:T(128)} %order_ref.1, bf16[32,3072]{1,0:T(8,128)(2,1)} %latents_ref.1, f32[3,16,3072]{2,1,0:T(8,128)} %bitcast.13, bf16[128,4,256]{2,1,0:T(4,128)(2,1)} %bitcast.14, bf16[3072,4,384]{2,1,0:T(4,128)(2,1)} %bitcast.9, ...), custom_call_target="tpu_custom_call" | custom-call | flops 4026531840 | bytes 31457280 | tf_op jit(solution)/shard_map/pallas_call | solution.py:545
  145.0 1.3 copy.12

commit v4 on v3

--- a/solution.py
+++ b/solution.py
@@ -218,7 +218,7 @@
     chunk = 256
     chunk_count = width // chunk
     hd = head_width // 3
-    pieces = [(0, cols)] if cols < 512 else [(0, cols - 256), (cols - 256, 256)]
+    pieces = [(0, cols)] if cols < 512 else [(0, 256), (256, cols - 256)]
     attn_width = heads * hd
     mlp_width = wi.shape[1]
     req_total = mod_ref.shape[1]
@@ -229,12 +229,12 @@
 
     for c in range(chunk_count):
         raw_load(c).start()
-    loads = [pltpu.make_async_copy(w_in_ref, wi, w_sem.at[0])]
-    late_loads = [
+    loads = [
+        pltpu.make_async_copy(w_in_ref, wi, w_sem.at[0]),
         pltpu.make_async_copy(w_attn_ref, wo.at[pl.ds(0, attn_width)], w_sem.at[1]),
         pltpu.make_async_copy(w_mlp_ref, wo.at[pl.ds(attn_width, mlp_width)], w_sem.at[2]),
     ]
-    for load in loads + late_loads:
+    for load in loads:
         load.start()
 
     barrier = pltpu.get_barrier_semaphore()
@@ -251,7 +251,6 @@
         return carry
 
     lax.fori_loop(1, devices, greet, 0)
-    pl.semaphore_wait(barrier, devices - 1)
 
     def peer(step):
         if reqs % 2:
@@ -270,12 +269,6 @@
             device_id_type=MESH,
         )
 
-    @pl.when(s == 0)
-    def _():
-        for step in range(1, reqs):
-            lat_copy(step).start()
-        lat[pl.ds(pl.multiple_of(r * own_rows, own_rows), own_rows), :] = latents_ref[...]
-
     place = lax.broadcasted_iota(jnp.int32, (patches, patches), 0)
     lane = lax.broadcasted_iota(jnp.int32, (patches, patches), 1)
     first, second = order_ref[0], order_ref[1]
@@ -295,16 +288,31 @@
         inside = (route >= start.astype(F32)) & (route < end.astype(F32))
         owner = jnp.where((req_lane == q) & inside, 1.0, owner)
         start = end
+    pl.semaphore_wait(barrier, devices - 1)
+
+    @pl.when(s == 0)
+    def _():
+        for step in range(1, reqs):
+            lat_copy(step).start()
+        lat[pl.ds(pl.multiple_of(r * own_rows, own_rows), own_rows), :] = latents_ref[...]
+
     same[...] = dot(owner, owner, ((1,), (1,)))
     chosen_bf = chosen.astype(F32).astype(BF16)
     stale = stale_ref[...].reshape(patches, heads * 2 * hd)
     stale = dot(chosen_bf[rows:, :], stale).astype(BF16)
     for h in range(heads):
         kv[h, rows:, :] = stale[:, h * 2 * hd : (h + 1) * 2 * hd]
+    owner_bf = owner.astype(BF16)
+    owners = jnp.concatenate([owner_bf, owner_bf, owner_bf], axis=1)
     for k in range(3):
         for c in range(reqs):
             at = pl.ds(c * cols, cols)
-            value = dot(owner, mod_ref[k, :, at], precision=lax.Precision.HIGHEST)
+            table = mod_ref[k, :, at]
+            high = table.astype(BF16)
+            left = table - high.astype(F32)
+            middle = left.astype(BF16)
+            low = (left - middle.astype(F32)).astype(BF16)
+            value = dot(owners, jnp.concatenate([high, middle, low], axis=0))
             mods[k, :, at] = value + 1.0 if k == 1 else value
 
     def flatten(c, carry):
@@ -314,6 +322,8 @@
         return carry
 
     lax.fori_loop(0, chunk_count, flatten, 0)
+    for load in loads:
+        load.wait()
 
     @pl.when(s == 0)
     def _():
@@ -351,13 +361,13 @@
 
         stats = []
         for p, (begin, size) in enumerate(pieces):
-            for q in range(reqs):
+            for step in range(reqs):
+                q = peer(step)
 
                 @pl.when(s > 0)
                 def _():
                     x_copy(p, t, q, q).wait_recv()
 
-            for q in range(reqs):
                 value = xin[t, q, :, begin : begin + size].astype(F32)
                 mean = jnp.sum(value, axis=1, keepdims=True) / size
                 value = value - mean
@@ -369,11 +379,6 @@
             at = pl.ds(c * cols, cols)
             value = (xin[t, c].astype(F32) - mean) * scale
             normed[:, at] = (value * mods[1, at_rows, at] + mods[0, at_rows, at]).astype(BF16)
-
-        @pl.when(t == 0)
-        def _():
-            for load in loads:
-                load.wait()
 
         allowed = same[at_rows, :] > 0.5
         group = 2 if heads % 2 == 0 else 1
@@ -417,18 +422,20 @@
             for h in range(heads):
                 act[:, h * hd : (h + 1) * hd] = dot(attention[h], kv[h, :, hd:]).astype(BF16)
 
-        @pl.when(t == 0)
-        def _():
-            for load in late_loads:
-                load.wait()
-
         for p, (begin, size) in enumerate(pieces):
-            for step in [*range(reqs - 1, 0, -1), 0]:
-                at = pl.ds(pl.multiple_of(peer(step) * cols + begin, 128), size)
-                product = dot(act[...], wo[:, at]).astype(BF16)
-                part_send[t, step, :, begin : begin + size] = product
-                if step > 0:
-                    part_copy(p, t, step).start()
+            together = 2 if size <= 256 and reqs % 2 == 0 else 1
+            for base in range(reqs - 1, -1, -together):
+                steps = range(base, base - together, -1)
+                ats = [pl.ds(pl.multiple_of(peer(m) * cols + begin, 128), size) for m in steps]
+                taken = [wo[:, at] for at in ats]
+                taken = jnp.concatenate(taken, axis=1) if together > 1 else taken[0]
+                product = dot(act[...], taken).astype(BF16)
+                for m, step in enumerate(steps):
+                    part_send[t, step, :, begin : begin + size] = product[
+                        :, m * size : (m + 1) * size
+                    ]
+                    if step > 0:
+                        part_copy(p, t, step).start()
         for p, (begin, size) in enumerate(pieces):
             branch = part_send[t, 0, :, begin : begin + size].astype(F32)
             for step in range(1, reqs):

time: 147 us -> 147 us (level)
  no operation moved by 1% of the time
where the time goes in v4:
time: 147 us
  Pallas kernels  145 us (99%)
    pallas_call x1, Pallas kernels, relay_shards(): pl.pallas_call(functools.partial(relay_kernel, sections, reqs), out_shape...  145 us

profile of v4, /device:TPU:1, one launch (start us, length us, event | category | flops | bytes accessed | tf_op | source)
XLA Modules:
  0.0 146.6 jit_solution(1518553344813942194)
XLA Ops:
  0.0 145.3 %shard_map.100 = bf16[32,384]{1,0:T(8,128)(2,1)} custom-call(s32[1,128]{1,0:T(1,128)} %bitcast.15, s32[16]{0:T(128)} %len_ref.1, s32[2]{0:T(128)} %order_ref.1, bf16[32,3072]{1,0:T(8,128)(2,1)} %latents_ref.1, f32[3,16,3072]{2,1,0:T(8,128)} %bitcast.13, bf16[128,4,256]{2,1,0:T(4,128)(2,1)} %bitcast.14, bf16[3072,4,384]{2,1,0:T(4,128)(2,1)} %bitcast.9, ...), custom_call_target="tpu_custom_call" | custom-call | flops 4026531840 | bytes 31457280 | tf_op jit(solution)/shard_map/pallas_call | solution.py:552
  145.3 1.3 copy.12

commit v5 on v4

--- a/solution.py
+++ b/solution.py
@@ -190,6 +190,8 @@
     same,
     perm,
     mods,
+    fixes,
+    early,
     part_send,
     part_recv,
     xnew,
@@ -304,16 +306,19 @@
         kv[h, rows:, :] = stale[:, h * 2 * hd : (h + 1) * 2 * hd]
     owner_bf = owner.astype(BF16)
     owners = jnp.concatenate([owner_bf, owner_bf, owner_bf], axis=1)
-    for k in range(3):
+
+    def expand(table):
+        high = table.astype(BF16)
+        left = table - high.astype(F32)
+        middle = left.astype(BF16)
+        low = (left - middle.astype(F32)).astype(BF16)
+        return dot(owners, jnp.concatenate([high, middle, low], axis=0))
+
+    for k in (1, 2):
         for c in range(reqs):
             at = pl.ds(c * cols, cols)
-            table = mod_ref[k, :, at]
-            high = table.astype(BF16)
-            left = table - high.astype(F32)
-            middle = left.astype(BF16)
-            low = (left - middle.astype(F32)).astype(BF16)
-            value = dot(owners, jnp.concatenate([high, middle, low], axis=0))
-            mods[k, :, at] = value + 1.0 if k == 1 else value
+            value = expand(mod_ref[k, :, at])
+            mods[k - 1, :, at] = value + 1.0 if k == 1 else value
 
     def flatten(c, carry):
         raw_load(c).wait()
@@ -324,6 +329,17 @@
     lax.fori_loop(0, chunk_count, flatten, 0)
     for load in loads:
         load.wait()
+    qkv_width = heads * head_width
+    group = 2 if heads % 2 == 0 else 1
+    span = group * head_width
+    piece = mlp_width // 3 if mlp_width % 384 == 0 else mlp_width
+    qkv_parts = [(wq, at, span, at) for at in range(0, qkv_width, span)]
+    mlp_parts = [(wi, at, piece, qkv_width + at) for at in range(0, mlp_width, piece)]
+    lines = jnp.concatenate([mod_ref[1] + 1.0, mod_ref[0]], axis=0).astype(BF16)
+    for weight, at, size, to in qkv_parts + mlp_parts:
+        lined = dot(lines, weight[:, at : at + size])
+        fixes[0, :, to : to + size] = expand(lined[:req_total])
+        fixes[1, :, to : to + size] = expand(lined[req_total:])
 
     @pl.when(s == 0)
     def _():
@@ -359,7 +375,19 @@
     def slot(t, carry):
         at_rows = pl.ds(pl.multiple_of(t * rows, rows), rows)
 
+        def push(p, part):
+            begin, size = pieces[p]
+            weight, at, part_size, _ = part
+            return sum(
+                dot(
+                    normed[:, c * cols + begin : c * cols + begin + size],
+                    weight[c * cols + begin : c * cols + begin + size, at : at + part_size],
+                )
+                for c in range(reqs)
+            )
+
         stats = []
+        base = None
         for p, (begin, size) in enumerate(pieces):
             for step in range(reqs):
                 q = peer(step)
@@ -372,31 +400,43 @@
                 mean = jnp.sum(value, axis=1, keepdims=True) / size
                 value = value - mean
                 stats.append((size, mean, jnp.sum(value * value, axis=1, keepdims=True)))
+            if base is None:
+                base = sum(part for _, part, _ in stats) / reqs
+            for c in range(reqs):
+                at = pl.ds(c * cols + begin, size)
+                value = xin[t, c, :, begin : begin + size].astype(F32) - base
+                normed[:, at] = (value * mods[0, at_rows, at]).astype(BF16)
+            if p < len(pieces) - 1:
+                for part in qkv_parts + mlp_parts:
+                    at = pl.ds(part[3], part[2])
+                    pushed = push(p, part)
+                    early[:, at] = pushed if p == 0 else early[:, at] + pushed
         mean = sum(size * part for size, part, _ in stats) / width
         square = sum(part + size * (at - mean) * (at - mean) for size, at, part in stats)
         scale = lax.rsqrt(square / width + 1e-06)
-        for c in range(reqs):
-            at = pl.ds(c * cols, cols)
-            value = (xin[t, c].astype(F32) - mean) * scale
-            normed[:, at] = (value * mods[1, at_rows, at] + mods[0, at_rows, at]).astype(BF16)
+        offset = mean - base
+
+        def product(part):
+            at = pl.ds(part[3], part[2])
+            value = push(len(pieces) - 1, part)
+            if len(pieces) > 1:
+                value = value + early[:, at]
+            return (value - offset * fixes[0, at_rows, at]) * scale + fixes[1, at_rows, at]
 
         allowed = same[at_rows, :] > 0.5
-        group = 2 if heads % 2 == 0 else 1
         queries = []
         for g in range(heads // group):
-            span = group * head_width
-            qkv = dot(normed[...], wq[:, g * span : (g + 1) * span])
+            qkv = product(qkv_parts[g])
             for h in range(group):
                 begin = h * head_width
                 queries.append(qkv[:, begin : begin + hd].astype(BF16))
                 fresh = qkv[:, begin + hd : begin + head_width].astype(BF16)
                 kv[g * group + h, at_rows, :] = fresh
 
-        piece = mlp_width // 3 if mlp_width % 384 == 0 else mlp_width
-        chunks = mlp_width // piece
+        chunks = len(mlp_parts)
 
         def up(c):
-            return dot(normed[...], wi[:, c * piece : (c + 1) * piece])
+            return product(mlp_parts[c])
 
         def keep(c, hidden):
             at = attn_width + c * piece
@@ -429,9 +469,9 @@
                 ats = [pl.ds(pl.multiple_of(peer(m) * cols + begin, 128), size) for m in steps]
                 taken = [wo[:, at] for at in ats]
                 taken = jnp.concatenate(taken, axis=1) if together > 1 else taken[0]
-                product = dot(act[...], taken).astype(BF16)
+                shares = dot(act[...], taken).astype(BF16)
                 for m, step in enumerate(steps):
-                    part_send[t, step, :, begin : begin + size] = product[
+                    part_send[t, step, :, begin : begin + size] = shares[
                         :, m * size : (m + 1) * size
                     ]
                     if step > 0:
@@ -442,7 +482,7 @@
                 part_copy(p, t, step).wait_recv()
                 branch = branch + part_recv[t, step, :, begin : begin + size].astype(F32)
             own = pl.ds(pl.multiple_of(r * cols + begin, 128), size)
-            gated = mods[2, at_rows, own] * branch
+            gated = mods[1, at_rows, own] * branch
             updated = xin[t, r, :, begin : begin + size].astype(F32) + gated
             xnew[t, :, begin : begin + size] = updated.astype(BF16)
 
@@ -566,7 +606,9 @@
             pltpu.VMEM((heads, patches, 2 * hd), BF16),
             pltpu.VMEM((patches, patches), F32),
             pltpu.VMEM((patches, patches), BF16),
-            pltpu.VMEM((3, patches, width), F32),
+            pltpu.VMEM((2, patches, width), F32),
+            pltpu.VMEM((2, patches, heads * head_width + mlp_width), F32),
+            pltpu.VMEM((rows, heads * head_width + mlp_width), F32),
             pltpu.VMEM((2, reqs, rows, cols), BF16),
             pltpu.VMEM((2, reqs, rows, cols), BF16),
             pltpu.VMEM((2, rows, cols), BF16),

time: 147 us -> 147 us (level)
  no operation moved by 1% of the time
where the time goes in v5:
time: 147 us; the launch traced here: 146 us
  Pallas kernels  145 us (99%)
    pallas_call x1, Pallas kernels, relay_shards(): pl.pallas_call(functools.partial(relay_kernel, sections, reqs), out_shape...  145 us

profile of v5, /device:TPU:1, one launch (start us, length us, event | category | flops | bytes accessed | tf_op | source)
XLA Modules:
  0.0 146.5 jit_solution(5203449822785201783)
XLA Ops:
  0.0 145.1 %shard_map.100 = bf16[32,384]{1,0:T(8,128)(2,1)} custom-call(s32[1,128]{1,0:T(1,128)} %bitcast.15, s32[16]{0:T(128)} %len_ref.1, s32[2]{0:T(128)} %order_ref.1, bf16[32,3072]{1,0:T(8,128)(2,1)} %latents_ref.1, f32[3,16,3072]{2,1,0:T(8,128)} %bitcast.13, bf16[128,4,256]{2,1,0:T(4,128)(2,1)} %bitcast.14, bf16[3072,4,384]{2,1,0:T(4,128)(2,1)} %bitcast.9, ...), custom_call_target="tpu_custom_call" | custom-call | flops 4026531840 | bytes 31457280 | tf_op jit(solution)/shard_map/pallas_call | solution.py:592
  145.2 1.3 copy.12

commit v6 on v5

--- a/solution.py
+++ b/solution.py
@@ -162,6 +162,11 @@
     return lax.dot_general(
         left, right, (dims, ((), ())), precision=precision, preferred_element_type=F32
     )
+
+
+def pieces_of(cols):
+    size = 256 if cols % 256 == 0 else cols
+    return [(begin, size) for begin in range(0, cols, size)]
 
 
 def relay_kernel(
@@ -220,7 +225,7 @@
     chunk = 256
     chunk_count = width // chunk
     hd = head_width // 3
-    pieces = [(0, cols)] if cols < 512 else [(0, 256), (256, cols - 256)]
+    pieces = pieces_of(cols)
     attn_width = heads * hd
     mlp_width = wi.shape[1]
     req_total = mod_ref.shape[1]
@@ -327,8 +332,7 @@
         return carry
 
     lax.fori_loop(0, chunk_count, flatten, 0)
-    for load in loads:
-        load.wait()
+    loads[0].wait()
     qkv_width = heads * head_width
     group = 2 if heads % 2 == 0 else 1
     span = group * head_width
@@ -340,6 +344,8 @@
         lined = dot(lines, weight[:, at : at + size])
         fixes[0, :, to : to + size] = expand(lined[:req_total])
         fixes[1, :, to : to + size] = expand(lined[req_total:])
+    for load in loads[1:]:
+        load.wait()
 
     @pl.when(s == 0)
     def _():
@@ -462,21 +468,20 @@
             for h in range(heads):
                 act[:, h * hd : (h + 1) * hd] = dot(attention[h], kv[h, :, hd:]).astype(BF16)
 
-        for p, (begin, size) in enumerate(pieces):
-            together = 2 if size <= 256 and reqs % 2 == 0 else 1
-            for base in range(reqs - 1, -1, -together):
-                steps = range(base, base - together, -1)
-                ats = [pl.ds(pl.multiple_of(peer(m) * cols + begin, 128), size) for m in steps]
-                taken = [wo[:, at] for at in ats]
-                taken = jnp.concatenate(taken, axis=1) if together > 1 else taken[0]
-                shares = dot(act[...], taken).astype(BF16)
-                for m, step in enumerate(steps):
-                    part_send[t, step, :, begin : begin + size] = shares[
-                        :, m * size : (m + 1) * size
-                    ]
-                    if step > 0:
-                        part_copy(p, t, step).start()
-        for p, (begin, size) in enumerate(pieces):
+        def share(p, steps):
+            begin, size = pieces[p]
+            ats = [pl.ds(pl.multiple_of(peer(m) * cols + begin, 128), size) for m in steps]
+            taken = [wo[:, at] for at in ats]
+            taken = jnp.concatenate(taken, axis=1) if len(steps) > 1 else taken[0]
+            shares = dot(act[...], taken).astype(BF16)
+            for m, step in enumerate(steps):
+                value = shares[:, m * size : (m + 1) * size]
+                part_send[t, step, :, begin : begin + size] = value
+                if step > 0:
+                    part_copy(p, t, step).start()
+
+        def update(p):
+            begin, size = pieces[p]
             branch = part_send[t, 0, :, begin : begin + size].astype(F32)
             for step in range(1, reqs):
                 part_copy(p, t, step).wait_recv()
@@ -490,6 +495,21 @@
             def _():
                 for step in range(reqs - 1, -1, -1):
                     x_copy(p, t, peer(step), r).start()
+
+        together = 2 if reqs % 2 == 0 else 1
+        turns = [
+            (p, list(range(last, last - together, -1)))
+            for p in range(len(pieces))
+            for last in range(reqs - 1, -1, -together)
+        ]
+        updated = 0
+        for n, (p, steps) in enumerate(turns):
+            if n == len(turns) - 1 and len(pieces) > 1:
+                update(0)
+                updated = 1
+            share(p, steps)
+        for p in range(updated, len(pieces)):
+            update(p)
 
         @pl.when(s == sections - 1)
         def _():
@@ -618,10 +638,10 @@
             pltpu.SemaphoreType.DMA((3 + width // 256,)),
             pltpu.SemaphoreType.DMA((reqs,)),
             pltpu.SemaphoreType.DMA((reqs,)),
-            pltpu.SemaphoreType.DMA((2, 2, reqs)),
-            pltpu.SemaphoreType.DMA((2, 2, reqs)),
-            pltpu.SemaphoreType.DMA((2, 2, reqs)),
-            pltpu.SemaphoreType.DMA((2, 2, reqs)),
+            pltpu.SemaphoreType.DMA((len(pieces_of(cols)), 2, reqs)),
+            pltpu.SemaphoreType.DMA((len(pieces_of(cols)), 2, reqs)),
+            pltpu.SemaphoreType.DMA((len(pieces_of(cols)), 2, reqs)),
+            pltpu.SemaphoreType.DMA((len(pieces_of(cols)), 2, reqs)),
             pltpu.SemaphoreType.DMA((per, reqs)),
             pltpu.SemaphoreType.DMA((1,)),
         ],

time: 147 us -> 138 us (0.939)
  Pallas kernels: 145 us -> 136 us
    pallas_call x1, Pallas kernels: 145 us -> 136 us  [relay_shards(): pl.pallas_call(functools.partial(relay_kernel, sections, reqs), out_shape...]
where the time goes in v6:
time: 138 us
  Pallas kernels  136 us (99%)
    pallas_call x1, Pallas kernels, relay_shards(): pl.pallas_call(functools.partial(relay_kernel, sections, reqs), out_shape...  136 us

profile of v6, /device:TPU:1, one launch (start us, length us, event | category | flops | bytes accessed | tf_op | source)
XLA Modules:
  0.0 137.7 jit_solution(5537214187861885917)
XLA Ops:
  0.0 136.4 %shard_map.100 = bf16[32,384]{1,0:T(8,128)(2,1)} custom-call(s32[1,128]{1,0:T(1,128)} %bitcast.15, s32[16]{0:T(128)} %len_ref.1, s32[2]{0:T(128)} %order_ref.1, bf16[32,3072]{1,0:T(8,128)(2,1)} %latents_ref.1, f32[3,16,3072]{2,1,0:T(8,128)} %bitcast.13, bf16[128,4,256]{2,1,0:T(4,128)(2,1)} %bitcast.14, bf16[3072,4,384]{2,1,0:T(4,128)(2,1)} %bitcast.9, ...), custom_call_target="tpu_custom_call" | custom-call | flops 4026531840 | bytes 31457280 | tf_op jit(solution)/shard_map/pallas_call | solution.py:612
  136.4 1.3 copy.12

commit v7 on v6

--- a/solution.py
+++ b/solution.py
@@ -504,7 +504,7 @@
         ]
         updated = 0
         for n, (p, steps) in enumerate(turns):
-            if n == len(turns) - 1 and len(pieces) > 1:
+            if n == len(turns) - 2 and len(pieces) > 2:
                 update(0)
                 updated = 1
             share(p, steps)

time: 138 us -> 141 us (1.022)
  Pallas kernels: 136 us -> 140 us
    pallas_call x1, Pallas kernels: 136 us -> 140 us  [relay_shards(): pl.pallas_call(functools.partial(relay_kernel, sections, reqs), out_shape...]
where the time goes in v7:
time: 141 us
  Pallas kernels  140 us (99%)
    pallas_call x1, Pallas kernels, relay_shards(): pl.pallas_call(functools.partial(relay_kernel, sections, reqs), out_shape...  140 us

profile of v7, /device:TPU:1, one launch (start us, length us, event | category | flops | bytes accessed | tf_op | source)
XLA Modules:
  0.0 141.2 jit_solution(6862683910465291189)
XLA Ops:
  0.0 139.8 %shard_map.100 = bf16[32,384]{1,0:T(8,128)(2,1)} custom-call(s32[1,128]{1,0:T(1,128)} %bitcast.15, s32[16]{0:T(128)} %len_ref.1, s32[2]{0:T(128)} %order_ref.1, bf16[32,3072]{1,0:T(8,128)(2,1)} %latents_ref.1, f32[3,16,3072]{2,1,0:T(8,128)} %bitcast.13, bf16[128,4,256]{2,1,0:T(4,128)(2,1)} %bitcast.14, bf16[3072,4,384]{2,1,0:T(4,128)(2,1)} %bitcast.9, ...), custom_call_target="tpu_custom_call" | custom-call | flops 4026531840 | bytes 31457280 | tf_op jit(solution)/shard_map/pallas_call | solution.py:612
  139.8 1.3 copy.12
